TPU v7x, 32 devices: a whole 2x2x4 slice. The times are simulated.
32 devices in a mesh: seq: 8 (over z, y), branch: 4 (over x, core).
Axes of the slice: x: 2, y: 2, z: 4, core: 2. Of those that a mesh axis runs over, the one named last changes fastest.
Arguments:
- q_ctl: bfloat16 [4, 1536, 2048], P('branch', 'seq'), may hold values from -64 to 64
- k_ctl: bfloat16 [4, 1536, 2048], P('branch', 'seq'), may hold values from -64 to 64
- v_ctl: bfloat16 [4, 1536, 2048], P('branch', 'seq'), may hold values from -6 to 6
- positions: int32 [1536], P('seq'), may hold values from 0 to 6143
- branch_ids: int32 [4], P('branch'), may hold values from 0 to 63
- cond_scale: float32 [64], replicated, may hold values from 0.25 to 2
- out_weight: bfloat16 [2048, 3072], P('branch', 'seq'), may hold values from -0.125 to 0.125
- frozen: bfloat16 [1536, 3072], P(('seq', 'branch')), may hold values from -2.390625 to 2.390625
- norm_gain: float32 [3072], replicated, may hold values from 0.5 to 1.5
- cotangent: bfloat16 [1536, 3072], P('seq'), may hold values from -6 to 6
Outputs:
- normed: bfloat16 [1536, 3072], P(('seq', 'branch'))
- grad_attn: bfloat16 [4, 1536, 2048], P('branch', 'seq')
All inputs are finite; a program needn't handle non-finite values.
Results may differ from a plain program's by a relative error of at most 0.014.
Values may be sent and summed in bfloat16 or wider, within the bound.
A program may use at most 64 MiB of HBM per device.

v0:
```python
import math

import jax
import jax.numpy as jnp
from jax import lax
from jax.sharding import PartitionSpec as P

HEADS = 16
HEAD_DIM = 128


EPS = 1e-06


def from_partner(shard, axis, distance):
    return lax.ppermute(shard, axis, [(i, i ^ 1 << distance) for i in range(lax.axis_size(axis))])


def rope_tables(positions, head_dim):
    exponents = jnp.arange(head_dim // 2, dtype=jnp.float32) * (2.0 / head_dim)
    frequencies = 10000.0 ** (-exponents)
    angles = positions.astype(jnp.float32)[..., None] * frequencies
    return (jnp.cos(angles), jnp.sin(angles))


def rotate(values_in, cosines, sines):
    half_dim = values_in.shape[-1] // 2
    front_half = values_in[..., :half_dim]
    back_half = values_in[..., half_dim:]
    return jnp.concatenate(
        [front_half * cosines - back_half * sines, back_half * cosines + front_half * sines],
        axis=-1,
    )


def normalize(hidden, norm_gain):
    inverse = lax.rsqrt(jnp.mean(hidden * hidden, axis=-1, keepdims=True) + EPS)
    return (hidden * inverse * norm_gain).astype(jnp.bfloat16)


def norm_grad(hidden, norm_gain, cotangent):
    inverse = lax.rsqrt(jnp.mean(hidden * hidden, axis=-1, keepdims=True) + EPS)
    upstream = cotangent.astype(jnp.float32) * norm_gain
    inner_mean = jnp.mean(upstream * hidden, axis=-1, keepdims=True)
    return (inverse * upstream - hidden * (inverse * inverse * inverse) * inner_mean).astype(
        jnp.bfloat16
    )


def attend_head(packed):
    query_rows, key_rows, value_rows = packed
    clip_len = query_rows.shape[0]
    block_rows = min(512, clip_len)
    factor = 1.0 / math.sqrt(query_rows.shape[-1])

    def one_block(query_block):
        scores = jnp.dot(query_block, key_rows.T, preferred_element_type=jnp.float32) * factor
        row_max = jnp.max(scores, axis=-1, keepdims=True)
        weights = jnp.exp(scores - row_max)
        row_total = jnp.sum(weights, axis=-1, keepdims=True)
        weights_low = (weights / row_total).astype(jnp.bfloat16)
        return jnp.dot(weights_low, value_rows, preferred_element_type=jnp.float32).astype(
            jnp.bfloat16
        )

    blocks = query_rows.reshape(clip_len // block_rows, block_rows, query_rows.shape[-1])
    return lax.map(one_block, blocks).reshape(clip_len, query_rows.shape[-1])


def regroup(buffer, group_bits, seq_index, forward):
    full_shape = buffer.shape
    split = buffer.reshape(full_shape[:1] + (2,) * group_bits + full_shape[2:])
    for bit in range(group_bits):
        axis_here = group_bits - bit
        mine = jnp.bitwise_and(jnp.right_shift(seq_index, bit), 1)
        other = 1 - mine
        outgoing = lax.dynamic_index_in_dim(split, other, axis_here, keepdims=True)
        if forward:
            incoming = from_partner(outgoing, "seq", bit)
        else:
            incoming = from_partner(outgoing, "seq", bit)
        split = lax.dynamic_update_index_in_dim(split, incoming, other, axis_here)
    return split.reshape(full_shape)


def on_device(
    q_ctl, k_ctl, v_ctl, positions, branch_ids, cond_scale, out_weight, frozen, norm_gain, cotangent
):
    branch_index = lax.axis_index("branch")
    quarters = lax.axis_size("branch")
    seq_index = lax.axis_index("seq")
    seq_devices = lax.axis_size("seq")
    group = min(HEADS, seq_devices)
    group_bits = group.bit_length() - 1
    local_len = q_ctl.shape[1]
    feature_width = q_ctl.shape[2]
    head_dim = HEAD_DIM
    head_count = feature_width // head_dim
    heads_here = head_count // group
    clip_len = group * local_len
    quarter_len = local_len // quarters
    model_width = cotangent.shape[1]
    cosines, sines = rope_tables(positions, head_dim)
    cosines = cosines[:, None, :]
    sines = sines[:, None, :]

    def heads_first(source, rotated):
        split_heads = source[0].reshape(local_len, head_count, head_dim)
        if rotated:
            split_heads = rotate(split_heads.astype(jnp.float32), cosines, sines).astype(
                jnp.bfloat16
            )
        split_heads = split_heads.reshape(local_len, group, heads_here, head_dim)
        return jnp.transpose(split_heads, (1, 0, 2, 3))

    stacked = jnp.stack(
        [heads_first(q_ctl, True), heads_first(k_ctl, True), heads_first(v_ctl, False)]
    )
    arrived = regroup(stacked, group_bits, seq_index, True)

    def per_head(member):
        return jnp.transpose(member, (2, 0, 1, 3)).reshape(heads_here, clip_len, head_dim)

    attended_heads = lax.map(
        attend_head, (per_head(arrived[0]), per_head(arrived[1]), per_head(arrived[2]))
    )
    going_back = jnp.transpose(
        attended_heads.reshape(heads_here, group, local_len, head_dim), (1, 2, 0, 3)
    )[None]
    returned = regroup(going_back, group_bits, seq_index, False)[0]
    attended = jnp.transpose(returned, (1, 0, 2, 3)).reshape(local_len, feature_width)
    branch_scale = jnp.sum(
        jnp.where(jnp.arange(cond_scale.shape[0]) == branch_ids[0], cond_scale, 0.0)
    )
    weight_rows = lax.all_gather(out_weight, "seq", axis=1, tiled=True)
    mixed = lax.psum_scatter(
        (branch_scale * attended.astype(jnp.float32)).astype(jnp.bfloat16),
        "branch",
        scatter_dimension=1,
        tiled=True,
    ).astype(jnp.float32)
    mixed_high = mixed.astype(jnp.bfloat16)
    mixed_rest = (mixed - mixed_high.astype(jnp.float32)).astype(jnp.bfloat16)
    partial_stream = jnp.dot(mixed_high, weight_rows, preferred_element_type=jnp.float32)
    partial_stream = partial_stream + jnp.dot(
        mixed_rest, weight_rows, preferred_element_type=jnp.float32
    )
    owner = (jnp.arange(quarters) == branch_index).astype(jnp.float32)[:, None, None]
    term = (
        partial_stream.reshape(quarters, quarter_len, model_width)
        + owner * frozen.astype(jnp.float32)[None]
    )
    hidden = (
        lax.psum(term.astype(jnp.bfloat16), "branch")
        .astype(jnp.float32)
        .reshape(local_len, model_width)
    )
    hidden_share = lax.dynamic_slice_in_dim(hidden, branch_index * quarter_len, quarter_len, 0)
    normed = normalize(hidden_share, norm_gain)
    grad_hidden = norm_grad(hidden, norm_gain, cotangent)
    cot_block = jnp.einsum(
        "td,hd->th", grad_hidden, weight_rows, preferred_element_type=jnp.float32
    ).astype(jnp.bfloat16)
    cot_attn = lax.all_gather(cot_block, "branch", axis=1, tiled=True)
    grad_attn = (branch_scale * cot_attn.astype(jnp.float32)).astype(jnp.bfloat16)
    return (normed, grad_attn.reshape(1, local_len, feature_width))


def solution(mesh):
    return jax.shard_map(
        on_device,
        mesh=mesh,
        in_specs=(
            P("branch", "seq", None),
            P("branch", "seq", None),
            P("branch", "seq", None),
            P("seq"),
            P("branch"),
            P(),
            P("branch", "seq"),
            P(("seq", "branch"), None),
            P(),
            P("seq", None),
        ),
        out_specs=(P(("seq", "branch"), None), P("branch", "seq", None)),
        check_vma=False,
    )
```

profile of v0, /device:TPU:0, one launch (start us, length us, event | category | flops | bytes accessed | tf_op | source)
XLA Modules:
  0.0 329.6 jit_solution(14406107373409805297)
XLA Ops:
  8.1 0.7 convert_element_type.82
  8.7 1.4 convert_bitcast_fusion.1
  11.3 1.1 subtract_convert_fusion.2
  12.4 2.1 maximum_bitcast_fusion
  14.8 2.1 maximum_bitcast_fusion.1
  16.9 1.1 copy.16
  18.6 1.1 copy.17
  19.7 1.6 pad_maximum_fusion
  21.3 1.1 constant_dynamic-slice_fusion.6
  22.4 2.9 collective-permute-start
  25.4 26.3 %collective-permute-done = bf16[3,2,2,1,192,2,128]{6,4,3,2,1,5,0:T(8,128)(2,1)} collective-permute-done((bf16[3,2,2,1,192,2,128]{6,4,3,2,1,5,0:T(8,128)(2,1)}, bf16[3,2,2,1,192,2,128]{6,4,3,2,1,5,0:T(8,128)(2,1)}, u32[]{:S(2)}, u32[]{:S(2)}) %collective-permute-start) | collective-permute-done | bytes 1179680 | tf_op jit(solution)/shard_map/ppermute | solution.py:16
  51.6 1.4 constant_dynamic-update-slice_fusion.5
  53.1 1.1 constant_dynamic-slice_fusion.5
  54.2 1.8 collective-permute-start.1
  56.0 25.6 %collective-permute-done.1 = bf16[3,2,1,2,192,2,128]{6,4,3,2,1,5,0:T(8,128)(2,1)} collective-permute-done((bf16[3,2,1,2,192,2,128]{6,4,3,2,1,5,0:T(8,128)(2,1)}, bf16[3,2,1,2,192,2,128]{6,4,3,2,1,5,0:T(8,128)(2,1)}, u32[]{:S(2)}, u32[]{:S(2)}) %collective-permute-start.1) | collective-permute-done | bytes 1179680 | tf_op jit(solution)/shard_map/ppermute | solution.py:16
  81.7 1.4 constant_dynamic-update-slice_fusion.4
  83.1 1.2 constant_dynamic-slice_fusion.4
  84.2 2.6 collective-permute-start.2
  87.1 84.7 %collective-permute-done.2 = bf16[3,1,2,2,192,2,128]{6,4,3,2,1,5,0:T(8,128)(2,1)} collective-permute-done((bf16[3,1,2,2,192,2,128]{6,4,3,2,1,5,0:T(8,128)(2,1)}, bf16[3,1,2,2,192,2,128]{6,4,3,2,1,5,0:T(8,128)(2,1)}, u32[]{:S(2)}, u32[]{:S(2)}) %collective-permute-start.2) | collective-permute-done | bytes 1179680 | tf_op jit(solution)/shard_map/ppermute | solution.py:16
  171.7 1.4 constant_dynamic-update-slice_fusion.3
  173.1 1.4 fusion.17
  174.5 18.3 %while.21 = (s32[]{:T(128)}, bf16[2,1536,128]{2,1,0:T(8,128)(2,1)}, bf16[2,1536,128]{2,1,0:T(8,128)(2,1)}, bf16[2,1536,128]{2,1,0:T(8,128)(2,1)}, bf16[2,1536,12...) while((s32[]{:T(128)}, bf16[2,1536,128]{2,1,0:T(8,128)(2,1)}, bf16[2,1536,128]{2,1,0:T(8,128)(2,1)}, ...), condition=%wide.region_6.7_spmd, body=%wide.region_1.6_spmd.sunk | while | flops 408222720 | bytes 19933468 | solution.py:124
  174.5 1.0 dynamic-slice_bitcast_fusion.3
  175.6 1.0 constant_dynamic-slice_fusion.8
  176.6 6.1 %while.22 = (s32[]{:T(128)}, bf16[3,512,128]{2,1,0:T(8,128)(2,1)S(1)}, bf16[3,512,128]{2,1,0:T(8,128)(2,1)S(1)}, bf16[1536,128]{1,0:T(8,128)(2,1)S(1)}, bf16[1536,128]{1,0:T(8,128)(2,1)S(1)}, /*index=5*/s32[]{:T(128)}) while((s32[]{:T(128)}, bf16[3,512,128]{2,1,0:T(8,128)(2,1)S(1)}, bf16[3,512,128]{2,1,0:T(8,128)(2,1)S(1)}, ...), condition=%wide.region_5.5_spmd, body=%wide.region_2.4_spmd.sunk | while | flops 408222720 | bytes 10496077 | solution.py:67
  176.6 0.7 fusion.32
  177.8 0.8 fusion.34
  178.6 0.7 fusion.32
  179.9 0.8 fusion.34
  180.7 0.7 fusion.32
  181.9 0.8 fusion.34
  182.8 0.9 copy-done.6
  183.6 1.0 dynamic-slice_bitcast_fusion.3
  184.7 1.0 constant_dynamic-slice_fusion.8
  185.7 6.1 %while.22 = (s32[]{:T(128)}, bf16[3,512,128]{2,1,0:T(8,128)(2,1)S(1)}, bf16[3,512,128]{2,1,0:T(8,128)(2,1)S(1)}, bf16[1536,128]{1,0:T(8,128)(2,1)S(1)}, bf16[1536,128]{1,0:T(8,128)(2,1)S(1)}, /*index=5*/s32[]{:T(128)}) while((s32[]{:T(128)}, bf16[3,512,128]{2,1,0:T(8,128)(2,1)S(1)}, bf16[3,512,128]{2,1,0:T(8,128)(2,1)S(1)}, ...), condition=%wide.region_5.5_spmd, body=%wide.region_2.4_spmd.sunk | while | flops 408222720 | bytes 10496077 | solution.py:67
  185.7 0.7 fusion.32
  187.0 0.8 fusion.34
  187.8 0.7 fusion.32
  189.0 0.8 fusion.34
  189.8 0.7 fusion.32
  191.0 0.8 fusion.34
  191.9 0.9 copy-done.6
  192.8 1.9 copy.19
  195.0 1.1 collective-permute-start.3
  196.1 6.7 %collective-permute-done.3 = bf16[1,2,2,1,192,2,128]{6,5,3,2,1,4,0:T(2,128)(2,1)S(1)} collective-permute-done((bf16[1,2,2,1,192,2,128]{6,5,3,2,1,4,0:T(2,128)(2,1)S(1)}, bf16[1,2,2,1,192,2,128]{6,5,3,2,1,4,0:T(2,128)(2,1)S(1)}, u32[]{:S(2)}, u32[]{:S(2)}) %collective-permute-start.3) | collective-permute-done | bytes 393248 | tf_op jit(solution)/shard_map/ppermute | solution.py:16
  203.7 4.5 %collective-permute-start.4 = (bf16[1,2,1,2,192,2,128]{6,5,3,2,1,4,0:T(2,128)(2,1)S(1)}, bf16[1,2,1,2,192,2,128]{6,5,3,2,1,4,0:T(2,128)(2,1)S(1)}, u32[]{:S(2)}, u32[]{:S(2)}) collective-permute-start(bf16[1,2,1,2,192,2,128]{6,5,3,2,1,4,0:T(2,128)(2,1)S(1)} %constant_dynamic-slice_fusion.2), channel_id=1, source_target_pairs={{0,8},{4,12},{8,0},{12,4},{16,24},{20,28},{24,16},{28,20},{1,9},{5... | collective-permute-start | bytes 1179656 | tf_op jit(solution)/shard_map/ppermute | solution.py:16
  208.2 8.2 %collective-permute-done.4 = bf16[1,2,1,2,192,2,128]{6,5,3,2,1,4,0:T(2,128)(2,1)S(1)} collective-permute-done((bf16[1,2,1,2,192,2,128]{6,5,3,2,1,4,0:T(2,128)(2,1)S(1)}, bf16[1,2,1,2,192,2,128]{6,5,3,2,1,4,0:T(2,128)(2,1)S(1)}, u32[]{:S(2)}, u32[]{:S(2)}) %collective-permute-start.4) | collective-permute-done | bytes 393248 | tf_op jit(solution)/shard_map/ppermute | solution.py:16
  217.1 3.4 %collective-permute-start.5 = (bf16[1,1,2,2,192,2,128]{6,5,3,2,1,4,0:T(2,128)(2,1)S(1)}, bf16[1,1,2,2,192,2,128]{6,5,3,2,1,4,0:T(2,128)(2,1)S(1)}, u32[]{:S(2)}, u32[]{:S(2)}) collective-permute-start(bf16[1,1,2,2,192,2,128]{6,5,3,2,1,4,0:T(2,128)(2,1)S(1)} %constant_dynamic-slice_fusion.1), channel_id=1, source_target_pairs={{0,16},{4,20},{8,24},{12,28},{16,0},{20,4},{24,8},{28,12},{1,17},{... | collective-permute-start | bytes 1179656 | tf_op jit(solution)/shard_map/ppermute | solution.py:16
  221.2 0.7 fusion.15
  221.8 14.6 %collective-permute-done.5 = bf16[1,1,2,2,192,2,128]{6,5,3,2,1,4,0:T(2,128)(2,1)S(1)} collective-permute-done((bf16[1,1,2,2,192,2,128]{6,5,3,2,1,4,0:T(2,128)(2,1)S(1)}, bf16[1,1,2,2,192,2,128]{6,5,3,2,1,4,0:T(2,128)(2,1)S(1)}, u32[]{:S(2)}, u32[]{:S(2)}) %collective-permute-start.5) | collective-permute-done | bytes 393248 | tf_op jit(solution)/shard_map/ppermute | solution.py:16
  236.8 1.2 multiply_convert_fusion.1
  238.0 1.5 convert_element_type.87
  239.6 0.9 convert_element_type.91
  240.5 23.5 %reduce-scatter.2.cloned.1.call-done = bf16[192,512]{1,0:T(8,128)(2,1)} async-done(((bf16[192,2048]{1,0:T(8,128)(2,1)}), bf16[192,512]{1,0:T(8,128)(2,1)}) %reduce-scatter.2.cloned.1.call-update) | async-done | bytes 196624 | tf_op jit(solution)/shard_map/reduce_scatter | solution.py:136
  263.9 2.8 fusion.18
  266.8 0.9 convolution_add_fusion
  267.9 1.3 add_convert_fusion
  269.2 37.2 %all-reduce.2.cloned.1.call-done = bf16[4,48,3072]{2,1,0:T(8,128)(2,1)} async-done(((bf16[4,48,3072]{2,1,0:T(8,128)(2,1)}), bf16[4,48,3072]{2,1,0:T(8,128)(2,1)}) %all-reduce.2.cloned.1.call-update) | async-done | bytes 1179664 | tf_op jit(solution)/shard_map/psum | solution.py:154
  306.5 1.6 multiply_reduce_fusion.1
  308.1 2.2 multiply_reduce_fusion
  310.4 1.3 fusion.13
  311.7 7.8 %all_gather.7 = bf16[192,2048]{1,0:T(8,128)(2,1)S(1)} all-gather(bf16[192,512]{1,0:T(8,128)(2,1)S(1)} %fusion.13), channel_id=1, replica_groups=mesh['seq'=8,'branch'=4] {'branch'}, dimensions={1}, use_global_device_ids=true | all-gather | bytes 983040 | tf_op jit(solution)/shard_map/all_gather | solution.py:164
  319.5 1.7 fusion.14
  321.3 0.8 multiply_convert_fusion.2
  (61 shorter events, 8.5 us)
Async XLA Ops:
  8.0 232.5 %all-gather.2.cloned.1.call-start = ((), (), s32[]{:S(2)}) async-start(), calls=%async_computation.2 | async-start | bytes 3538944 | tf_op jit(solution)/shard_map/all_gather | solution.py:135
  8.7 1.7 copy-start.7
  14.8 3.2 copy-start.4
  22.4 29.2 %collective-permute-start = (bf16[3,2,2,1,192,2,128]{6,4,3,2,1,5,0:T(8,128)(2,1)}, bf16[3,2,2,1,192,2,128]{6,4,3,2,1,5,0:T(8,128)(2,1)}, u32[]{:S(2)}, u32[]{:S(2)}) collective-permute-start(bf16[3,2,2,1,192,2,128]{6,4,3,2,1,5,0:T(8,128)(2,1)} %constant_dynamic-slice_fusion.6), channel_id=1, source_target_pairs={{0,4},{4,0},{8,12},{12,8},{16,20},{20,16},{24,28},{28,24},{1,5},{5... | collective-permute-start | bytes 3538952 | tf_op jit(solution)/shard_map/ppermute | solution.py:16
  54.2 27.5 %collective-permute-start.1 = (bf16[3,2,1,2,192,2,128]{6,4,3,2,1,5,0:T(8,128)(2,1)}, bf16[3,2,1,2,192,2,128]{6,4,3,2,1,5,0:T(8,128)(2,1)}, u32[]{:S(2)}, u32[]{:S(2)}) collective-permute-start(bf16[3,2,1,2,192,2,128]{6,4,3,2,1,5,0:T(8,128)(2,1)} %constant_dynamic-slice_fusion.5), channel_id=1, source_target_pairs={{0,8},{4,12},{8,0},{12,4},{16,24},{20,28},{24,16},{28,20},{1,9},{5... | collective-permute-start | bytes 3538952 | tf_op jit(solution)/shard_map/ppermute | solution.py:16
  84.2 87.5 %collective-permute-start.2 = (bf16[3,1,2,2,192,2,128]{6,4,3,2,1,5,0:T(8,128)(2,1)}, bf16[3,1,2,2,192,2,128]{6,4,3,2,1,5,0:T(8,128)(2,1)}, u32[]{:S(2)}, u32[]{:S(2)}) collective-permute-start(bf16[3,1,2,2,192,2,128]{6,4,3,2,1,5,0:T(8,128)(2,1)} %constant_dynamic-slice_fusion.4), channel_id=1, source_target_pairs={{0,16},{4,20},{8,24},{12,28},{16,0},{20,4},{24,8},{28,12},{1,17},{... | collective-permute-start | bytes 3538952 | tf_op jit(solution)/shard_map/ppermute | solution.py:16
  86.8 177.1 %reduce-scatter.2.cloned.1.call-start = ((), (), s32[]{:S(2)}) async-start(), calls=%async_computation.1 | async-start | bytes 983040 | tf_op jit(solution)/shard_map/reduce_scatter | solution.py:136
  176.6 6.1 %copy-start.5 = (bf16[2,1536,128]{2,1,0:T(8,128)(2,1)S(1)}, bf16[2,1536,128]{2,1,0:T(8,128)(2,1)}, u32[]{:S(2)}) copy-start(bf16[2,1536,128]{2,1,0:T(8,128)(2,1)} %get-tuple-element.206) | copy-start | bytes 2359300 | tf_op jit(solution)/shard_map/while
  182.7 0.9 copy-start.6
  185.7 6.1 %copy-start.5 = (bf16[2,1536,128]{2,1,0:T(8,128)(2,1)S(1)}, bf16[2,1536,128]{2,1,0:T(8,128)(2,1)}, u32[]{:S(2)}) copy-start(bf16[2,1536,128]{2,1,0:T(8,128)(2,1)} %get-tuple-element.206) | copy-start | bytes 2359300 | tf_op jit(solution)/shard_map/while
  191.9 0.9 copy-start.6
  194.7 26.4 %copy-start.10 = (f32[64]{0:T(128)S(1)}, f32[64]{0:T(128)}, u32[]{:S(2)}) copy-start(f32[64]{0:T(128)} %param.19) | copy-start | bytes 772
  195.0 7.8 %collective-permute-start.3 = (bf16[1,2,2,1,192,2,128]{6,5,3,2,1,4,0:T(2,128)(2,1)S(1)}, bf16[1,2,2,1,192,2,128]{6,5,3,2,1,4,0:T(2,128)(2,1)S(1)}, u32[]{:S(2)}, u32[]{:S(2)}) collective-permute-start(bf16[1,2,2,1,192,2,128]{6,5,3,2,1,4,0:T(2,128)(2,1)S(1)} %constant_dynamic-slice_fusion.3), channel_id=1, source_target_pairs={{0,4},{4,0},{8,12},{12,8},{16,20},{20,16},{24,28},{28,24},{1,5},{5... | collective-permute-start | bytes 1179656 | tf_op jit(solution)/shard_map/ppermute | solution.py:16
  203.7 12.7 %collective-permute-start.4 = (bf16[1,2,1,2,192,2,128]{6,5,3,2,1,4,0:T(2,128)(2,1)S(1)}, bf16[1,2,1,2,192,2,128]{6,5,3,2,1,4,0:T(2,128)(2,1)S(1)}, u32[]{:S(2)}, u32[]{:S(2)}) collective-permute-start(bf16[1,2,1,2,192,2,128]{6,5,3,2,1,4,0:T(2,128)(2,1)S(1)} %constant_dynamic-slice_fusion.2), channel_id=1, source_target_pairs={{0,8},{4,12},{8,0},{12,4},{16,24},{20,28},{24,16},{28,20},{1,9},{5... | collective-permute-start | bytes 1179656 | tf_op jit(solution)/shard_map/ppermute | solution.py:16
  217.1 19.3 %collective-permute-start.5 = (bf16[1,1,2,2,192,2,128]{6,5,3,2,1,4,0:T(2,128)(2,1)S(1)}, bf16[1,1,2,2,192,2,128]{6,5,3,2,1,4,0:T(2,128)(2,1)S(1)}, u32[]{:S(2)}, u32[]{:S(2)}) collective-permute-start(bf16[1,1,2,2,192,2,128]{6,5,3,2,1,4,0:T(2,128)(2,1)S(1)} %constant_dynamic-slice_fusion.1), channel_id=1, source_target_pairs={{0,16},{4,20},{8,24},{12,28},{16,0},{20,4},{24,8},{28,12},{1,17},{... | collective-permute-start | bytes 1179656 | tf_op jit(solution)/shard_map/ppermute | solution.py:16
  221.8 17.8 %copy-start.8 = (bf16[48,3072]{1,0:T(8,128)(2,1)S(1)}, bf16[48,3072]{1,0:T(8,128)(2,1)}, u32[]{:S(2)}) copy-start(bf16[48,3072]{1,0:T(8,128)(2,1)} %param.21) | copy-start | bytes 884740
  239.5 66.9 %all-reduce.2.cloned.1.call-start = ((), (), s32[]{:S(2)}) async-start(), calls=%async_computation.3 | async-start | bytes 2359296 | tf_op jit(solution)/shard_map/psum | solution.py:154
  240.5 26.3 %copy-start = (bf16[512,3072]{1,0:T(8,128)(2,1)S(1)}, bf16[512,3072]{1,0:T(8,128)(2,1)}, u32[]{:S(2)}) copy-start(bf16[512,3072]{1,0:T(8,128)(2,1)} %all-gather.2.cloned.1.call-done) | copy-start | bytes 9437188
  263.9 2.8 copy-start.3
  266.8 1.1 copy-start.1
  267.9 40.3 %copy-start.9 = (f32[3072]{0:T(1024)S(1)}, f32[3072]{0:T(1024)}, u32[]{:S(2)}) copy-start(f32[3072]{0:T(1024)} %param.22) | copy-start | bytes 36868
  308.1 2.2 copy-start.2
Sparse Core Ops, SparseCore 0:
  86.9 88.2 all-gather.1
Sparse Core Ops, SparseCore 1:
  239.6 24.3 reduce-scatter.1
  269.3 37.1 all-reduce.1
where the time goes:
time: 330 us
  waiting for transfers between devices  227 us (69%)
  local copies, waits for them, and re-layouts  24.4 us (7%)
  other arithmetic  23.6 us (7%)
  starting transfers between devices  16.7 us (5%)
  between operations  16.4 us (5%)
  matrix products  13.6 us (4%)
  blocking collectives  7.83 us (2%)
    ppermute x6, waiting for transfers between devices, from_partner(): lax.ppermute(shard, axis, [(i, i ^ 1 << distance) for i in range(lax.axis...  166 us
    psum x1, waiting for transfers between devices, on_device(): lax.psum(term.astype(jnp.bfloat16), 'branch').astype(jnp.float32)  37.2 us
    reduce_scatter x1, waiting for transfers between devices, on_device(): lax.psum_scatter((branch_scale * attended.astype(jnp.float32)).astype(jnp...  23.5 us
    ppermute x6, starting transfers between devices, from_partner(): lax.ppermute(shard, axis, [(i, i ^ 1 << distance) for i in range(lax.axis...  16.4 us
    all_gather x1, blocking collectives, on_device(): cot_attn = lax.all_gather(cot_block, 'branch', axis=1, tiled=True)  7.83 us
  transfers between devices with their start and end apart: 9, of which 8 were waited for; matrix products, arithmetic and copies ran while one was open for 8% of the time, Pallas kernels for 0%

commit v1 on v0

v1 whole, which is shorter than its diff:
```python
import functools
import math

import jax
import jax.numpy as jnp
from jax import lax
from jax.experimental import pallas as pl
from jax.experimental.pallas import tpu as pltpu
from jax.sharding import PartitionSpec as P

HEADS = 16
HEAD_DIM = 128
EPS = 1e-06
MESH = pl.DeviceIdType.MESH
F32 = jnp.float32
BF16 = jnp.bfloat16


def remote(src, dst, send_sem, recv_sem, target):
    return pltpu.make_async_remote_copy(
        src_ref=src, dst_ref=dst, send_sem=send_sem, recv_sem=recv_sem,
        device_id=target, device_id_type=MESH,
    )


def aligned(index, size):
    return pl.ds(pl.multiple_of(index * size, size), size)


def attend_kernel(
    group, nb, q_ref, k_ref, v_ref, cos_ref, sin_ref, scale_ref, out_ref,
    qs, ks, qr, kr, vr, obuf, osum, msend, mrow, mcol,
    s_in, r_in, s_sum, r_sum, s_back, r_back, s_turn, r_turn,
):
    c = lax.axis_index("branch")
    seq = lax.axis_index("seq")
    i = lax.rem(seq, group)
    base = seq - i
    rows = q_ref.shape[0]
    part = rows // nb
    hd = HEAD_DIM
    hh = qr.shape[0]
    clip = qr.shape[1]
    width = mcol.shape[1]
    order = list(range(group - 1, 0, -1))

    def seq_peer(d):
        return base + jnp.bitwise_xor(i, d)

    def branch_peer(d):
        return jnp.bitwise_xor(c, d)

    barrier = pltpu.get_barrier_semaphore()
    for d in order:
        pl.semaphore_signal(barrier, inc=1, device_id={"seq": seq_peer(d)}, device_id_type=MESH)
    for d in range(1, nb):
        pl.semaphore_signal(barrier, inc=1, device_id={"branch": branch_peer(d)}, device_id_type=MESH)
    pl.semaphore_wait(barrier, group - 1 + nb - 1)

    cosines = cos_ref[...]
    sines = sin_ref[...]

    def rotate(src, cols):
        x = src[:, cols].astype(F32)
        return (x * cosines + pltpu.roll(x, hd // 2, 1) * sines).astype(BF16)

    mine = aligned(i, rows)
    sends = []
    arrivals = [[] for _ in range(hh)]

    def send_in(kind, h, d, src, dst):
        copy = remote(src, dst, s_in.at[kind, h, d], r_in.at[kind, h, d], {"seq": seq_peer(d)})
        copy.start()
        sends.append(copy)
        arrivals[h].append(copy)

    for h in range(hh):
        for d in order:
            cols = aligned(jnp.bitwise_xor(i, d) * hh + h, hd)
            send_in(2, h, d, v_ref.at[:, cols], vr.at[h, mine, :])
            ks[:, cols] = rotate(k_ref, cols)
            send_in(1, h, d, ks.at[:, cols], kr.at[h, mine, :])
            qs[:, cols] = rotate(q_ref, cols)
            send_in(0, h, d, qs.at[:, cols], qr.at[h, mine, :])
        cols = aligned(i * hh + h, hd)
        vr[h, mine, :] = v_ref[:, cols]
        kr[h, mine, :] = rotate(k_ref, cols)
        qr[h, mine, :] = rotate(q_ref, cols)

    factor = (1.0 / math.sqrt(hd)) * math.log2(math.e)
    scale = scale_ref[0, 0]
    block = rows
    sums = [[] for _ in range(hh)]
    for h in range(hh):
        for copy in arrivals[h]:
            copy.wait_recv()

        def one_block(n, carry, h=h):
            q = qr[h, aligned(n, block), :]
            s = lax.dot_general(q, kr[h], (((1,), (1,)), ((), ())), preferred_element_type=F32)
            top = jnp.max(s, axis=-1, keepdims=True)
            p = jnp.exp2((s - top) * factor)
            total = jnp.sum(p, axis=-1, keepdims=True)
            o = jnp.dot(p.astype(BF16), vr[h], preferred_element_type=F32)
            obuf[h, n] = (o * (scale / total)).astype(BF16)
            return carry

        lax.fori_loop(0, clip // block, one_block, 0)
        for d in range(nb - 1, 0, -1):
            copy = remote(
                obuf.at[h, :, aligned(branch_peer(d), part), :], osum.at[h, d - 1],
                s_sum.at[h, d], r_sum.at[h, d], {"branch": branch_peer(d)},
            )
            copy.start()
            sends.append(copy)
            sums[h].append(copy)

    backs = []
    for h in range(hh):
        for copy in sums[h]:
            copy.wait_recv()
        total = obuf[h, :, aligned(c, part), :].astype(F32)
        for d in range(1, nb):
            total = total + osum[h, d - 1].astype(F32)
        msend[h] = total.astype(BF16)
        cols = aligned(i * hh + h, hd)
        for d in order:
            copy = remote(
                msend.at[h, jnp.bitwise_xor(i, d)], mrow.at[:, cols],
                s_back.at[h, d], r_back.at[h, d], {"seq": seq_peer(d)},
            )
            copy.start()
            sends.append(copy)
            backs.append(copy)
        mrow[:, cols] = msend[h, i]
    for copy in backs:
        copy.wait_recv()

    turns = []
    for d in range(nb - 1, 0, -1):
        copy = remote(
            mrow.at[:, aligned(branch_peer(d), width)], mcol.at[aligned(c, part), :],
            s_turn.at[d], r_turn.at[d], {"branch": branch_peer(d)},
        )
        copy.start()
        sends.append(copy)
        turns.append(copy)
    mcol[aligned(c, part), :] = mrow[:, aligned(c, width)]
    for copy in turns:
        copy.wait_recv()
    out_ref[...] = mcol[...]
    for copy in sends:
        copy.wait_send()


def norm_kernel(
    chunks, m_ref, w_ref, frozen_ref, gain_ref, cot_ref, scale_ref, normed_ref, grad_ref,
    part, ra, sx, rx, hid, gh, cb,
    s_a, r_a, s_x, r_x, s_g, r_g, s_c, r_c,
):
    c = lax.axis_index("branch")
    near = jnp.bitwise_xor(c, 1)
    far = jnp.bitwise_xor(c, 2)
    across = jnp.bitwise_xor(c, 3)
    to_near = {"branch": near}
    to_far = {"branch": far}
    rows = m_ref.shape[0]
    quarter = frozen_ref.shape[0]
    depth, model = w_ref.shape
    step = model // chunks
    spans = [pl.ds(n * step, step) for n in range(chunks)]

    barrier = pltpu.get_barrier_semaphore()
    for target in (to_near, to_far):
        pl.semaphore_signal(barrier, inc=1, device_id=target, device_id_type=MESH)
    pl.semaphore_wait(barrier, 2)

    sends = []

    def send(src, dst, send_sem, recv_sem, target):
        copy = remote(src, dst, send_sem, recv_sem, target)
        copy.start()
        sends.append(copy)
        return copy

    first = []
    for n, span in enumerate(spans):
        part[:, span] = jnp.dot(
            m_ref[...], w_ref[:, span], preferred_element_type=F32
        ).astype(BF16)
        a = send(part.at[aligned(across, quarter), span], ra.at[1, :, span], s_a.at[1, n], r_a.at[1, n], to_near)
        b = send(part.at[aligned(near, quarter), span], ra.at[0, :, span], s_a.at[0, n], r_a.at[0, n], to_near)
        first.append((b, a))
    second = []
    for n, span in enumerate(spans):
        first[n][1].wait_recv()
        sx[:, span] = (
            part[aligned(far, quarter), span].astype(F32) + ra[1, :, span].astype(F32)
        ).astype(BF16)
        second.append(send(sx.at[:, span], rx.at[:, span], s_x.at[n], r_x.at[n], to_far))
    for n, span in enumerate(spans):
        first[n][0].wait_recv()
        hid[:, span] = (
            part[aligned(c, quarter), span].astype(F32)
            + ra[0, :, span].astype(F32)
            + frozen_ref[:, span].astype(F32)
        )
    square = jnp.zeros((quarter, 1), F32)
    inner = jnp.zeros((quarter, 1), F32)
    for n, span in enumerate(spans):
        second[n].wait_recv()
        value = hid[:, span] + rx[:, span].astype(F32)
        hid[:, span] = value
        up = cot_ref[aligned(c, quarter), span].astype(F32) * gain_ref[:, span]
        square = square + jnp.sum(value * value, axis=-1, keepdims=True)
        inner = inner + jnp.sum(up * value, axis=-1, keepdims=True)
    r = lax.rsqrt(square * (1.0 / model) + EPS)
    bend = r * r * r * (inner * (1.0 / model))
    own_far, own_near = [], []
    for n, span in enumerate(spans):
        up = cot_ref[aligned(c, quarter), span].astype(F32) * gain_ref[:, span]
        mine = gh.at[aligned(c, quarter), span]
        gh[aligned(c, quarter), span] = (r * up - hid[:, span] * bend).astype(BF16)
        own_far.append(send(mine, mine, s_g.at[0, n], r_g.at[0, n], to_far))
        own_near.append(send(mine, mine, s_g.at[1, n], r_g.at[1, n], to_near))
    for span in spans:
        normed_ref[:, span] = (hid[:, span] * r * gain_ref[:, span]).astype(BF16)
    passed = []
    for n, span in enumerate(spans):
        own_far[n].wait_recv()
        block = gh.at[aligned(far, quarter), span]
        passed.append(send(block, block, s_g.at[2, n], r_g.at[2, n], to_near))
    total = jnp.zeros((rows, depth), F32)
    for n, span in enumerate(spans):
        own_near[n].wait_recv()
        passed[n].wait_recv()
        total = total + lax.dot_general(
            gh[:, span], w_ref[:, span], (((1,), (1,)), ((), ())), preferred_element_type=F32
        )
    cb[c] = total.astype(BF16)
    out_far = send(cb.at[c], cb.at[c], s_c.at[0], r_c.at[0], to_far)
    out_near = send(cb.at[c], cb.at[c], s_c.at[1], r_c.at[1], to_near)
    scale = scale_ref[0, 0]

    def put(index):
        grad_ref[:, aligned(index, depth)] = (scale * cb[index].astype(F32)).astype(BF16)

    put(c)
    out_near.wait_recv()
    put(near)
    out_far.wait_recv()
    out_pass = send(cb.at[far], cb.at[far], s_c.at[2], r_c.at[2], to_near)
    put(far)
    out_pass.wait_recv()
    put(across)
    for copy in sends:
        copy.wait_send()


def on_device(
    q_ctl, k_ctl, v_ctl, positions, branch_ids, cond_scale, out_weight, frozen, norm_gain, cotangent
):
    nb = lax.axis_size("branch")
    group = min(HEADS, lax.axis_size("seq"))
    rows, features = q_ctl.shape[1:]
    hh = HEADS // group
    clip = group * rows
    part = rows // nb
    model = cotangent.shape[1]
    depth = features // nb
    hd = HEAD_DIM
    exponents = jnp.arange(hd // 2, dtype=F32) * (2.0 / hd)
    frequencies = 10000.0 ** (-exponents)
    angles = positions.astype(F32)[:, None] * frequencies
    cosines, sines = jnp.cos(angles), jnp.sin(angles)
    cosines = jnp.concatenate([cosines, cosines], axis=-1)
    sines = jnp.concatenate([-sines, sines], axis=-1)
    scale = jnp.sum(
        jnp.where(jnp.arange(cond_scale.shape[0]) == branch_ids[0], cond_scale, 0.0)
    ).reshape(1, 1)
    weight = lax.all_gather(out_weight, "seq", axis=1, tiled=True)
    vmem = pl.BlockSpec(memory_space=pltpu.VMEM)
    smem = pl.BlockSpec(memory_space=pltpu.SMEM)
    dma = pltpu.SemaphoreType.DMA
    mixed = pl.pallas_call(
        functools.partial(attend_kernel, group, nb),
        out_shape=jax.ShapeDtypeStruct((rows, depth), BF16),
        in_specs=[vmem] * 5 + [smem],
        out_specs=vmem,
        scratch_shapes=[
            pltpu.VMEM((rows, features), BF16),
            pltpu.VMEM((rows, features), BF16),
            pltpu.VMEM((hh, clip, hd), BF16),
            pltpu.VMEM((hh, clip, hd), BF16),
            pltpu.VMEM((hh, clip, hd), BF16),
            pltpu.VMEM((hh, group, rows, hd), BF16),
            pltpu.VMEM((hh, nb - 1, group, part, hd), BF16),
            pltpu.VMEM((hh, group, part, hd), BF16),
            pltpu.VMEM((part, features), BF16),
            pltpu.VMEM((rows, depth), BF16),
            dma((3, hh, group)), dma((3, hh, group)),
            dma((hh, nb)), dma((hh, nb)),
            dma((hh, group)), dma((hh, group)),
            dma((nb,)), dma((nb,)),
        ],
        compiler_params=pltpu.CompilerParams(
            collective_id=0, has_side_effects=True, vmem_limit_bytes=40 << 20
        ),
        cost_estimate=pl.CostEstimate(
            flops=4 * hh * clip * clip * hd, bytes_accessed=6 * rows * features,
            transcendentals=hh * clip * clip,
        ),
        name="attend",
    )(q_ctl[0], k_ctl[0], v_ctl[0], cosines, sines, scale)
    chunks = 4 if model % (4 * 128) == 0 else 1
    normed, grad = pl.pallas_call(
        functools.partial(norm_kernel, chunks),
        out_shape=(
            jax.ShapeDtypeStruct((part, model), BF16),
            jax.ShapeDtypeStruct((rows, features), BF16),
        ),
        in_specs=[vmem] * 5 + [smem],
        out_specs=(vmem, vmem),
        scratch_shapes=[
            pltpu.VMEM((rows, model), BF16),
            pltpu.VMEM((2, part, model), BF16),
            pltpu.VMEM((part, model), BF16),
            pltpu.VMEM((part, model), BF16),
            pltpu.VMEM((part, model), F32),
            pltpu.VMEM((rows, model), BF16),
            pltpu.VMEM((nb, rows, depth), BF16),
            dma((2, chunks)), dma((2, chunks)),
            dma((chunks,)), dma((chunks,)),
            dma((3, chunks)), dma((3, chunks)),
            dma((3,)), dma((3,)),
        ],
        compiler_params=pltpu.CompilerParams(
            collective_id=1, has_side_effects=True, vmem_limit_bytes=40 << 20
        ),
        cost_estimate=pl.CostEstimate(
            flops=4 * rows * model * depth, bytes_accessed=2 * model * depth, transcendentals=0
        ),
        name="inject",
    )(mixed, weight, frozen, norm_gain.reshape(1, model), cotangent, scale)
    return (normed, grad.reshape(1, rows, features))


def solution(mesh):
    return jax.shard_map(
        on_device,
        mesh=mesh,
        in_specs=(
            P("branch", "seq", None),
            P("branch", "seq", None),
            P("branch", "seq", None),
            P("seq"),
            P("branch"),
            P(),
            P("branch", "seq"),
            P(("seq", "branch"), None),
            P(),
            P("seq", None),
        ),
        out_specs=(P(("seq", "branch"), None), P("branch", "seq", None)),
        check_vma=False,
    )
```

time: 330 us -> 169 us (0.51)
  waiting for transfers between devices: 227 us -> 0.7 us
  Pallas kernels: 0 us -> 144 us
  other arithmetic: 23.6 us -> 2.5 us
  local copies, waits for them, and re-layouts: 24.4 us -> 6.88 us
  starting transfers between devices: 16.7 us -> 0.04 us
  matrix products: 13.6 us -> 0 us
  blocking collectives: 7.83 us -> 0 us
    ppermute x6 -> x0, waiting for transfers between devices: 166 us -> none  [from_partner(): lax.ppermute(shard, axis, [(i, i ^ 1 << distance) for i in range(lax.axis...]
    pallas_call x0 -> x2, Pallas kernels: none -> 144 us  [the longest x1 115 us: on_device(): pl.pallas_call(functools.partial(attend_kernel, group, nb), out_shape=jax...]
    psum x1 -> x0, waiting for transfers between devices: 37.2 us -> none  [on_device(): lax.psum(term.astype(jnp.bfloat16), 'branch').astype(jnp.float32)]
    reduce_scatter x1 -> x0, waiting for transfers between devices: 23.5 us -> none  [on_device(): lax.psum_scatter((branch_scale * attended.astype(jnp.float32)).astype(jnp...]
    ppermute x6 -> x0, starting transfers between devices: 16.4 us -> none  [from_partner(): lax.ppermute(shard, axis, [(i, i ^ 1 << distance) for i in range(lax.axis...]
    dot_general x15 -> x0, matrix products: 13.6 us -> none  [the longest x6 4.64 us: one_block(): jnp.dot(weights_low, value_rows, preferred_element_type=jnp.float32)]
    all_gather x1 -> x0, blocking collectives: 7.83 us -> none  [on_device(): cot_attn = lax.all_gather(cot_block, 'branch', axis=1, tiled=True)]
    reduce_sum x9 -> x0, other arithmetic: 7.37 us -> none  [the longest x6 3.44 us: one_block(): row_total = jnp.sum(weights, axis=-1, keepdims=True)]
  transfers between devices with their start and end apart: 9 -> 1, of which waited for: 8 -> 0; matrix products, arithmetic and copies ran while one was open for 8% -> 1% of each run, Pallas kernels for 0% -> 68%
where the time goes in v1:
time: 169 us
  Pallas kernels  144 us (85%)
  between operations  14.8 us (9%)
  local copies, waits for them, and re-layouts  6.88 us (4%)
  other arithmetic  2.5 us (1%)
    pallas_call x1, Pallas kernels, on_device(): pl.pallas_call(functools.partial(attend_kernel, group, nb), out_shape=jax...  115 us
    pallas_call x1, Pallas kernels, on_device(): pl.pallas_call(functools.partial(norm_kernel, chunks), out_shape=(jax.Sha...  28.7 us
    unnamed x16, local copies, waits for them, and re-layouts  6.88 us
  transfers between devices with their start and end apart: 1, of which 0 were waited for; matrix products, arithmetic and copies ran while one was open for 1% of the time, Pallas kernels for 68%

profile of v1, /device:TPU:0, one launch (start us, length us, event | category | flops | bytes accessed | tf_op | source)
XLA Modules:
  0.0 168.9 jit_solution(6483056671049170776)
XLA Ops:
  7.2 0.0 all-gather.2.cloned.1.call-start
  7.2 0.7 all-gather.2.cloned.1.call-update
  8.5 0.7 convert_element_type.3
  9.2 1.3 fusion.1
  10.5 0.4 fusion
  10.9 0.1 pad_maximum_fusion
  11.1 0.0 copy-start.4
  11.1 1.1 copy-done.4
  12.2 0.0 copy-start.5
  12.2 1.1 copy-done.5
  13.3 0.0 copy-start.6
  13.3 1.1 copy-done.6
  14.5 0.0 copy-start.1
  14.5 0.0 copy-start.2
  14.5 0.0 copy-start.3
  14.5 115.3 %attend.1.m_ref = bf16[192,512]{1,0:T(8,128)(2,1)S(1)} custom-call(bf16[192,2048]{1,0:T(8,128)(2,1)S(1)} %bitcast.10, bf16[192,2048]{1,0:T(8,128)(2,1)S(1)} %bitcast.11, bf16[192,2048]{1,0:T(8,128)(2,1)S(1)} %bitcast.12, f32[192,128]{1,0:T(8,128)S(1)} %get-tuple-element.9.cos_ref, f32[192,128]{1,0:T(8,128)S(1)} %get-tuple-element.10.sin_ref, ...), custom_call_target="tpu_custom_call" | custom-call | flops 2415919104 | bytes 2359296 | tf_op jit(solution)/shard_map/attend/pallas_call | solution.py:285
  129.8 0.0 all-gather.2.cloned.1.call-done.w_ref
  129.8 0.0 copy-done.1
  129.8 0.0 copy-done.2
  129.8 0.0 copy-done.3
  129.8 0.0 copy-start
  129.9 1.9 %copy-done = bf16[512,3072]{1,0:T(8,128)(2,1)S(1)} copy-done((bf16[512,3072]{1,0:T(8,128)(2,1)S(1)}, bf16[512,3072]{1,0:T(8,128)(2,1)}, u32[]{:S(2)}) %copy-start) | copy-done | bytes 3145752
  131.7 28.7 %inject.1 = (bf16[48,3072]{1,0:T(8,128)(2,1)S(1)}, bf16[192,2048]{1,0:T(8,128)(2,1)S(1)}) custom-call(bf16[192,512]{1,0:T(8,128)(2,1)S(1)} %attend.1.m_ref, bf16[512,3072]{1,0:T(8,128)(2,1)S(1)} %copy-done, bf16[48,3072]{1,0:T(8,128)(2,1)S(1)} %copy-done.2, f32[1,3072]{1,0:T(1,128)S(1)} %bitcast.9, bf16[192,3072]{1,0:T(8,128)(2,1)S(1)} %copy-done.1, ...), custom_call_target="tpu_custom_call" | custom-call | flops 1207959552 | bytes 3145728 | tf_op jit(solution)/shard_map/inject/pallas_call | solution.py:316
  160.5 0.7 copy.15
  161.2 0.9 copy.16
  (1 shorter events, 0.0 us)
Async XLA Ops:
  7.2 122.6 %all-gather.2.cloned.1.call-start = ((), (), s32[]{:S(2)}) async-start(), calls=%async_computation | async-start | bytes 3538944 | tf_op jit(solution)/shard_map/all_gather | solution.py:281
  11.1 1.1 copy-start.4
  12.2 1.1 copy-start.5
  13.3 1.1 copy-start.6
  14.5 115.4 %copy-start.1 = (bf16[192,3072]{1,0:T(8,128)(2,1)S(1)}, bf16[192,3072]{1,0:T(8,128)(2,1)}, u32[]{:S(2)}) copy-start(bf16[192,3072]{1,0:T(8,128)(2,1)} %cot_ref.1) | copy-start | bytes 3538948
  14.5 115.4 %copy-start.2 = (bf16[48,3072]{1,0:T(8,128)(2,1)S(1)}, bf16[48,3072]{1,0:T(8,128)(2,1)}, u32[]{:S(2)}) copy-start(bf16[48,3072]{1,0:T(8,128)(2,1)} %frozen_ref.1) | copy-start | bytes 884740
  14.5 115.4 %copy-start.3 = (f32[3072]{0:T(1024)S(1)}, f32[3072]{0:T(1024)}, u32[]{:S(2)}) copy-start(f32[3072]{0:T(1024)} %param.18) | copy-start | bytes 36868
  129.8 1.9 %copy-start = (bf16[512,3072]{1,0:T(8,128)(2,1)S(1)}, bf16[512,3072]{1,0:T(8,128)(2,1)}, u32[]{:S(2)}) copy-start(bf16[512,3072]{1,0:T(8,128)(2,1)} %all-gather.2.cloned.1.call-done.w_ref) | copy-start | bytes 9437188
Sparse Core Ops, SparseCore 0:
  10.1 103.0 all-gather.1
